TPU v7x, 32 devices: a whole 2x2x4 slice. The times are simulated.
32 devices in a mesh: real: 2 (over y), slab: 4 (over z), pencil: 2 (over x), sub: 2 (over core).
Axes of the slice: x: 2, y: 2, z: 4, core: 2. Of those that a mesh axis runs over, the one named last changes fastest.
Arguments:
- permeability: float32 [128, 64, 256], P(('real', 'slab'), ('pencil', 'sub')), parts along dimension 0, may hold values from 0.1 to 10
- source: float32 [128, 64, 256], P(('real', 'slab'), ('pencil', 'sub')), parts along dimension 0, may hold values from -24 to 24
- pressure: float32 [128, 64, 256], P(('real', 'slab'), ('pencil', 'sub')), parts along dimension 0, may hold values from -24 to 24
- aggregate: int32 [128], P('real'), parts along dimension 0, may hold values from 0 to 31, as said below
Outputs:
- pressure_out: float32 [128, 64, 256], P(('real', 'slab'), ('pencil', 'sub')), parts along dimension 0
There are 2 independent parts, one for each index of `real`. A program takes and returns all parts, laid end to end along the dimension named above; each array names one. Nothing has to cross between parts.
Inputs may be any that keep to these rules, and one draw needn't show every extreme that they name: `aggregate`: never falls along its dimension; each value covers 1 to 4 consecutive positions, some value exactly 4; positions k * 16 - 1 and k * 16 always hold the same value.
All inputs are finite; a program needn't handle non-finite values.
Results may differ from a plain program's by a relative error of at most 0.000068.
Values sent between devices are 32-bit elements; how exact they have to be, the bound alone decides.
A program may use at most 64 MiB of HBM per device.

v0:
```python
import functools
import jax
import jax.numpy as jnp
from jax import lax
from jax.experimental import pallas as pl
from jax.experimental.pallas import tpu as pltpu
from jax.sharding import PartitionSpec as P

OMEGA = 0.8
GRANT = 62 * 2**20
MESH = pl.DeviceIdType.MESH

DIRS = [(dx, dy) for dx in (1, 0, -1) for dy in (1, 0, -1) if (dx, dy) != (0, 0)]
FROM = {0: 0, 1: 1, -1: 2}


def dot(a, b):
    return jnp.dot(a, b, preferred_element_type=jnp.float32)


def halves(v):
    upper = v.astype(jnp.bfloat16)
    return upper, (v - upper.astype(jnp.float32)).astype(jnp.bfloat16)


def kernel(
    agg, k_in, s_in, p_in, out,
    ke, se, pe, khalo, shalo, phalo, fx, fy, fz, dg, wt, p1, p2, rr, rhalo,
    kpack, ppack, spack, edge, xhalo, result, fields, cm, cl, cr, cs, cmp, csp, hm, hl, hr, ext, corr, local_sem, send_sem, recv_sem,
):
    f32 = jnp.float32
    width = 16
    slab, slabs = lax.axis_index("slab"), lax.axis_size("slab")
    subs = lax.axis_size("sub")
    rows = lax.axis_size("pencil") * subs
    row = lax.axis_index("pencil") * subs + lax.axis_index("sub")

    loads = [
        pltpu.make_async_copy(src, dst.at[3:19, 0:16], local_sem.at[i])
        for i, (src, dst) in enumerate(((k_in, ke), (p_in, pe), (s_in, se)))
    ]
    for load in loads:
        load.start()

    def exists(dx, dy):
        ok = None
        for pos, step, count in ((slab, dx, slabs), (row, dy, rows)):
            if step:
                here = (pos + step < count) if step > 0 else (pos > 0)
                ok = here if ok is None else jnp.logical_and(ok, here)
        return ok

    def device(dx, dy):
        r = row + dy
        return {"slab": slab + dx, "pencil": r // subs, "sub": r % subs}

    barrier = pltpu.get_barrier_semaphore()
    for dx, dy in DIRS:
        @pl.when(exists(dx, dy))
        def _():
            pl.semaphore_signal(barrier, inc=1, device_id=device(dx, dy), device_id_type=MESH)
    near_x = 1 + (slab > 0).astype(jnp.int32) + (slab < slabs - 1).astype(jnp.int32)
    near_y = 1 + (row > 0).astype(jnp.int32) + (row < rows - 1).astype(jnp.int32)

    def message(kind, d, src, dst):
        return pltpu.make_async_remote_copy(
            src_ref=src, dst_ref=dst,
            send_sem=send_sem.at[kind * 8 + d], recv_sem=recv_sem.at[kind * 8 + d],
            device_id=device(*DIRS[d]), device_id_type=MESH,
        )

    def fine_message(kind, d, body, packed, halo, wide):
        dx, dy = DIRS[d]
        if dy == 0:
            src0 = 19 - wide if dx > 0 else 3
            dst0 = 3 - wide if dx > 0 else 19
            return message(kind, d, body.at[src0:src0 + wide, 0:16], body.at[dst0:dst0 + wide, 0:16])
        src0, dst0, length = {0: (1, 1, 8), 1: (9, 0, 1), -1: (0, 9, 1)}[dx]
        return message(
            kind, d, packed.at[FROM[dy] - 1, src0:src0 + length],
            halo.at[FROM[dy] - 1, dst0:dst0 + length],
        )

    def coarse_message(kind, d, q0, q1):
        dx, dy = DIRS[d]
        if dy == 0:
            qs = pl.ds(q0, q1 - q0)
            if dx > 0:
                return message(kind, d, cs.at[qs], cl.at[qs])
            return message(kind, d, cm.at[qs, 0:32], cr.at[qs])
        here = FROM[dy] - 1
        if q0 == 0:
            if dx > 0:
                return message(kind, d, cs.at[0], hl.at[here, 2])
            if dx < 0:
                return message(kind, d, cm.at[0, 0:32], hr.at[here, 2])
            return message(kind, d, cmp.at[here, 2, 0:64], hm.at[here, 2, 0:64])
        if dx > 0:
            return message(kind, d, csp.at[here], hl.at[here, 0:2])
        if dx < 0:
            return message(kind, d, cmp.at[here, 0:2, 0:32], hr.at[here, 0:2])
        return message(kind, d, cmp.at[here, 0:2], hm.at[here, 0:2])

    def post_message(d):
        dx, dy = DIRS[d]
        if dx > 0:
            return message(5, d, rr.at[18, 0:16], xhalo.at[0])
        if dx < 0:
            return message(5, d, rr.at[3, 0:16], xhalo.at[1])
        return message(5, d, edge.at[FROM[dy] - 1], rhalo.at[FROM[dy] - 1])

    kinds = {
        "k": lambda d: fine_message(0, d, ke, kpack, khalo, 3),
        "p": lambda d: fine_message(1, d, pe, ppack, phalo, 3),
        "s": lambda d: fine_message(2, d, se, spack, shalo, 2),
        "coef": lambda d: coarse_message(3, d, 1, 5),
        "rhs": lambda d: coarse_message(4, d, 0, 1),
        "post": post_message,
    }

    def each(name):
        return [d for d in range(8) if name != "post" or 0 in DIRS[d]]

    def send(name):
        for d in each(name):
            @pl.when(exists(*DIRS[d]))
            def _():
                kinds[name](d).start()

    def receive(name):
        for d in each(name):
            dx, dy = DIRS[d]
            @pl.when(exists(-dx, -dy))
            def _():
                kinds[name](d).wait_recv()

    def sent(name):
        for d in each(name):
            @pl.when(exists(*DIRS[d]))
            def _():
                kinds[name](d).wait_send()

    low_half = lax.broadcasted_iota(jnp.int32, (1, 8, 256), 1) < 4
    low_coarse = lax.broadcasted_iota(jnp.int32, (1, 8, 128), 1) < 4

    def turned(v):
        return pltpu.roll(v, 4, 1)

    def pair_up(a, b, low):
        return jnp.where(low, turned(b), a), jnp.where(low, a, turned(b))

    def pair_off(up, down, low):
        return jnp.where(low, down, up), turned(jnp.where(low, up, down))

    def pack(body, packed):
        for at, a, b, count in ((1, 3, 11, 8), (0, 3, 4, 1), (9, 17, 18, 1)):
            for way, lo in ((0, 8), (1, 0)):
                tiles = pair_up(body[a:a + count, lo:lo + 8], body[b:b + count, lo:lo + 8], low_half)
                packed[way, at:at + count] = tiles[way]

    for name, load, parts in zip("kps", loads, ((ke, kpack), (pe, ppack), (se, spack))):
        load.wait()
        pack(*parts)
        if name == "k":
            pl.semaphore_wait(barrier, near_x * near_y - 1)
        send(name)

    def clear(ref, *index):
        view = ref.at[index]
        view[...] = jnp.zeros(view.shape, f32)

    for ref in (ke, pe):
        clear(ref, 0, slice(16, 24))
        clear(ref, 21, slice(16, 24))
    clear(rr, 2)
    clear(rr, 19)
    for dx, dy in DIRS:
        @pl.when(jnp.logical_not(exists(-dx, -dy)))
        def _():
            if dx == 0:
                clear(rhalo, FROM[dy] - 1)
            if dy == 0:
                clear(xhalo, 0 if dx > 0 else 1)
            for ref, halo, wide in ((ke, khalo, 3), (pe, phalo, 3), (se, shalo, 2)):
                if dy == 0:
                    at = slice(3 - wide, 3) if dx > 0 else slice(19, 19 + wide)
                    clear(ref, at, slice(0, 16))
                else:
                    lo, hi = {0: (1, 9), 1: (0, 1), -1: (9, 10)}[dx]
                    clear(halo, FROM[dy] - 1, slice(lo, hi))
            if dy == 0:
                clear({1: cl, -1: cr}[dx])
            else:
                clear({0: hm, 1: hl, -1: hr}[dx], FROM[dy] - 1)

    y_at = lax.broadcasted_iota(jnp.int32, (24, 256), 0)
    z_at = lax.broadcasted_iota(jnp.int32, (24, 256), 1)
    y_rel = jnp.where(y_at < 20, y_at, y_at - 24)
    y_glob = y_rel + row * width
    ends_yz = (
        (y_glob == 0).astype(f32) + (y_glob == rows * width - 1).astype(f32)
        + (z_at == 0).astype(f32) + (z_at == 255).astype(f32)
    )
    odd_y = (y_at & 1) == 1
    odd_z = (z_at & 1) == 1

    def loop(lo, hi, step, unroll=4):
        def run(i, carry):
            step(i)
            return carry
        lax.fori_loop(lo, hi, run, 0, unroll=unroll)

    def set_rim(body, halo):
        for at, a, b, count in ((1, 3, 11, 8), (0, 1, 2, 1), (9, 19, 20, 1)):
            here = slice(at, at + count)
            first, second = pair_off(halo[0, here], halo[1, here], low_half)
            body[a:a + count, 16:24] = first
            body[b:b + count, 16:24] = second

    def next_y(v):
        return pltpu.roll(v, 23, 0)

    def prev_y(v):
        return pltpu.roll(v, 1, 0)

    def next_z(v):
        return pltpu.roll(v, 255, 1)

    def prev_z(v):
        return pltpu.roll(v, 1, 1)

    def face(a, b):
        total = a + b
        return 2.0 * a * b / jnp.where(total > 0, total, 1.0)

    ids = [agg[slab * width + x] for x in range(width)]
    slots = [i - ids[0] for i in ids]
    live = slots[15]
    col = lax.broadcasted_iota(jnp.int32, (1, 256), 1)
    slot_col = jnp.zeros((1, 256), jnp.int32)
    for x in range(width):
        inside = (col >> 4) == x
        slot_col = jnp.where(inside, slots[x], slot_col)
    r168 = lax.broadcasted_iota(jnp.int32, (168, 256), 0)
    c168 = lax.broadcasted_iota(jnp.int32, (168, 256), 1)
    want = jnp.where(r168 < 128, r168 >> 3, (r168 >> 3) - 20 + live)
    gather = ((want == slot_col) & ((r168 & 7) == ((c168 & 15) >> 1))).astype(f32)
    gather = jnp.concatenate([gather, gather], axis=1).astype(jnp.bfloat16)
    zr = lax.broadcasted_iota(jnp.int32, (512, 128), 0)
    zc = lax.broadcasted_iota(jnp.int32, (512, 128), 1)
    pair_z = (((zr & 255) >> 1) == zc).astype(f32).astype(jnp.bfloat16)

    def coarsen(q0, q1):
        count = q1 - q0
        flat = fields[q0:q1].reshape(count * 256, 256)
        pairs = dot(jnp.concatenate(halves(flat), axis=1), pair_z)
        pairs = jnp.concatenate([pairs[256 * q:256 * (q + 1)] for q in range(count)], axis=1)
        sums = dot(gather, jnp.concatenate(halves(pairs), axis=0))
        for q in range(count):
            part = sums[:, 128 * q:128 * (q + 1)]
            cm[q0 + q] = part[0:128]
            cs[q0 + q] = part[128:168]

    def pack_coarse(packed, pair, a, b):
        tiles = pair_up(a.reshape(-1, 8, 128), b.reshape(-1, 8, 128), low_coarse)
        for way in range(2):
            packed[way, pair, 0:a.shape[0]] = tiles[way].reshape(a.shape)

    receive("k")
    set_rim(ke, khalo)

    def x_faces(i):
        fx[i] = face(ke[i], ke[i + 1])
    loop(0, 21, x_faces)

    def other_faces(i):
        k = ke[i]
        north = face(k, next_y(k))
        above = jnp.where(z_at == 255, 0.0, face(k, next_z(k)))
        south, below = prev_y(north), prev_z(above)
        x_glob = slab * width + i - 3
        ends_x = (x_glob == 0).astype(f32) + (x_glob == slabs * width - 1).astype(f32)
        bound = 2.0 * k * (ends_yz + ends_x)
        fy[i] = north
        fz[i] = above
        diag = fx[i - 1] + fx[i] + north + south + above + below + bound
        dg[i] = diag
        wt[i] = OMEGA / jnp.where(diag > 0, diag, 1.0)
        return north, above, south, below, bound

    def plain_faces(i):
        other_faces(i)

    def own_faces(i):
        north, above, south, below, bound = other_faces(i)
        x = slab * width + i - 3
        crossing = agg[x] != agg[jnp.minimum(x + 1, slabs * width - 1)]
        fields[1, i - 3] = fx[i, 0:16] * crossing.astype(f32)
        fields[2, i - 3] = jnp.where(odd_y, north, 0.0)[0:16]
        fields[3, i - 3] = jnp.where(odd_z, above, 0.0)[0:16]
        whole = bound + jnp.where(odd_y, north, south) + jnp.where(odd_z, above, below)
        fields[4, i - 3] = whole[0:16]

    loop(3, 19, own_faces)
    coarsen(1, 5)
    for pair, q in ((0, 1), (1, 3)):
        pack_coarse(cmp, pair, cm[q], cm[q + 1])
        pack_coarse(csp, pair, cs[q], cs[q + 1])
    send("coef")
    loop(1, 3, plain_faces)
    loop(19, 21, plain_faces)

    def beside(src, i):
        v = src[i]
        north, above = fy[i], fz[i]
        around = fx[i - 1] * src[i - 1] + fx[i] * src[i + 1]
        around = around + (north * next_y(v) + prev_y(north * v))
        return v, around + (above * next_z(v) + prev_z(above * v))

    def sweep(src, dst, lo, hi):
        def step(i):
            v, around = beside(src, i)
            dst[i] = (1.0 - OMEGA) * v + wt[i] * (se[i] + around)
        loop(lo, hi, step)

    receive("p")
    set_rim(pe, phalo)
    receive("s")
    set_rim(se, shalo)
    sweep(pe, p1, 1, 21)
    sweep(p1, p2, 2, 20)

    def residual(i):
        v, around = beside(p2, i)
        fields[0, i - 3] = (se[i] - dg[i] * v + around)[0:16]
    loop(3, 19, residual)
    coarsen(0, 1)
    pack_coarse(cmp, 2, cm[0, 0:64], cm[0, 64:128])
    send("rhs")

    rp = lax.broadcasted_iota(jnp.int32, (384, 64), 0)
    cp = lax.broadcasted_iota(jnp.int32, (384, 64), 1)
    place = (((rp >> 4) - (cp >> 4) == 4 + live) & ((rp & 15) == (cp & 15))).astype(f32)
    place = jnp.concatenate([place, place], axis=1).astype(jnp.bfloat16)

    def joined(part, halo, q, count):
        own = part[q].reshape(count, 8, 128)
        if q > 0:
            pair = (q - 1) // 2
            tiles = [halo[way, pair].reshape(count, 8, 128) for way in range(2)]
            rim = pair_off(*tiles, low_coarse)[(q - 1) % 2]
        elif count == 16:
            tiles = [halo[way, 2, 0:64].reshape(8, 8, 128) for way in range(2)]
            rim = jnp.concatenate(pair_off(*tiles, low_coarse), axis=0)
        else:
            tiles = [halo[way, 2].reshape(count, 8, 128) for way in range(2)]
            rim = pair_off(*tiles, low_coarse)[0]
        return jnp.concatenate([own, rim], axis=1)

    def extend(q0, q1):
        count = q1 - q0
        ahead = [joined(cr, hr, q, 4).reshape(64, 128) for q in range(q0, q1)]
        after = dot(place, jnp.concatenate(halves(jnp.concatenate(ahead, axis=1)), axis=0))
        for q in range(q0, q1):
            at = 128 * (q - q0)
            ext[q] = after[:, at:at + 128].reshape(24, 16, 128)
            ext[q, 0:5] += joined(cl, hl, q, 5)
            ext[q, 4:20] += joined(cm, hm, q, 16)

    receive("coef")
    extend(1, 5)
    zl = lax.broadcasted_iota(jnp.int32, (16, 128), 1)
    def diagonal(t):
        diag = ext[4, t] + ext[1, t] + ext[1, t - 1]
        corr[2, t] = OMEGA / jnp.where(diag > 0, diag, 1.0)
    loop(1, 23, diagonal)
    ru = lax.broadcasted_iota(jnp.int32, (24, 256), 0)
    cu = lax.broadcasted_iota(jnp.int32, (24, 256), 1)
    same_y = (cu & 15) == jnp.where(ru < 20, ru >> 1, (ru >> 1) + 4)
    spread = jnp.concatenate(
        [(same_y & ((cu >> 4) == slots[x])).astype(f32) for x in range(width)], axis=0
    )
    er = lax.broadcasted_iota(jnp.int32, (256, 256), 0)
    ec = lax.broadcasted_iota(jnp.int32, (256, 256), 1)
    twice_z = ((ec >> 1) == (er & 127)).astype(f32).astype(jnp.bfloat16)
    receive("rhs")
    extend(0, 1)

    def first(t):
        corr[0, t] = corr[2, t] * ext[0, t]
    loop(1, 23, first)
    for number, (lo, hi) in enumerate(((2, 22), (3, 21), (4, 20))):
        src, dst = number % 2, (number + 1) % 2
        def coarse_sweep(t):
            v = corr[src, t]
            north, above = ext[2, t], ext[3, t]
            around = ext[1, t] * corr[src, t + 1] + ext[1, t - 1] * corr[src, t - 1]
            around = around + (north * pltpu.roll(v, 15, 0) + pltpu.roll(north * v, 1, 0))
            around = around + (above * pltpu.roll(v, 127, 1) + pltpu.roll(above * v, 1, 1))
            corr[dst, t] = (1.0 - OMEGA) * v + corr[2, t] * (ext[0, t] + around)
        loop(lo, hi, coarse_sweep)

    coarse = jnp.concatenate(halves(corr[1, 4:20].reshape(256, 128)), axis=1)
    fine = dot(dot(spread.astype(jnp.bfloat16), coarse).astype(jnp.bfloat16), twice_z)
    fine = fine.reshape(16, 24, 256)
    p1[3:19] = p2[3:19] + fine
    p1[2] = p2[2] + fine[0]
    p1[19] = p2[19] + fine[15]
    sweep(p1, rr, 3, 19)
    edge[0] = rr[3:19, 15, :]
    edge[1] = rr[3:19, 0, :]
    send("post")
    clear(rr, slice(3, 19), slice(16, 24))

    def last(i):
        v, around = beside(rr, i)
        result[i - 3] = ((1.0 - OMEGA) * v + wt[i] * (se[i] + around))[0:16]
    loop(3, 19, last)
    south = wt[3:19, 0, :] * fy[3:19, 23, :]
    north = wt[3:19, 15, :] * fy[3:19, 15, :]
    receive("post")
    result[0] += (wt[3, 0:16] * fx[2, 0:16]) * xhalo[0]
    result[15] += (wt[18, 0:16] * fx[18, 0:16]) * xhalo[1]
    result[:, 0, :] = result[:, 0, :] + south * rhalo[0]
    result[:, 15, :] = result[:, 15, :] + north * rhalo[1]
    store = pltpu.make_async_copy(result, out, local_sem.at[0])
    store.start()
    for name in kinds:
        sent(name)
    store.wait()


def body(permeability, source, pressure, aggregate):
    f32 = jnp.float32
    shape = permeability.shape
    block = pltpu.VMEM((22, 24, 256), f32)
    halo = pltpu.VMEM((2, 10, 8, 256), f32)
    hbm = pl.BlockSpec(memory_space=pltpu.HBM)
    return pl.pallas_call(
        kernel,
        out_shape=jax.ShapeDtypeStruct(shape, f32),
        in_specs=[pl.BlockSpec(memory_space=pltpu.SMEM), hbm, hbm, hbm],
        out_specs=hbm,
        scratch_shapes=[block, block, block, halo, halo, halo]
        + [block] * 8
        + [
            pltpu.VMEM((2, 16, 256), f32),
            halo,
            halo,
            halo,
            pltpu.VMEM((2, 16, 256), f32),
            pltpu.VMEM((2, 16, 256), f32),
            pltpu.VMEM((16, 16, 256), f32),
            pltpu.VMEM((5, 16, 16, 256), f32),
            pltpu.VMEM((5, 128, 128), f32),
            pltpu.VMEM((5, 40, 128), f32),
            pltpu.VMEM((5, 32, 128), f32),
            pltpu.VMEM((5, 40, 128), f32),
            pltpu.VMEM((2, 3, 128, 128), f32),
            pltpu.VMEM((2, 2, 40, 128), f32),
            pltpu.VMEM((2, 3, 128, 128), f32),
            pltpu.VMEM((2, 3, 40, 128), f32),
            pltpu.VMEM((2, 3, 32, 128), f32),
            pltpu.VMEM((5, 24, 16, 128), f32),
            pltpu.VMEM((3, 24, 16, 128), f32),
            pltpu.SemaphoreType.DMA((3,)),
            pltpu.SemaphoreType.DMA((48,)),
            pltpu.SemaphoreType.DMA((48,)),
        ],
        compiler_params=pltpu.CompilerParams(
            collective_id=0, has_side_effects=True, vmem_limit_bytes=GRANT
        ),
    )(aggregate, permeability, source, pressure)

def solution(mesh):
    spec = P(("real", "slab"), ("pencil", "sub"), None)
    return jax.shard_map(
        body, mesh=mesh, in_specs=(spec, spec, spec, P("real")), out_specs=spec, check_vma=False
    )
```

profile of v0, /device:TPU:0, one launch (start us, length us, event | category | flops | bytes accessed | tf_op | source)
XLA Modules:
  0.0 25.9 jit_solution(18164979121438112754)
XLA Ops:
  0.0 24.2 %shard_map.46 = f32[16,16,256]{2,1,0:T(8,128)} custom-call(s32[64]{0:T(128)} %agg.1, f32[16,16,256]{2,1,0:T(8,128)} %k_in.1, f32[16,16,256]{2,1,0:T(8,128)} %s_in.1, f32[16,16,256]{2,1,0:T(8,128)} %p_in.1), custom_call_target="tpu_custom_call" | custom-call | tf_op jit(solution)/shard_map/pallas_call | solution.py:439
  24.2 1.7 %copy.6 = f32[16,16,256]{2,1,0:T(8,128)} copy(f32[16,16,256]{2,1,0:T(8,128)} %shard_map.46) | data formatting | bytes 524288
where the time goes:
time: 26.1 us; the launch traced here: 25.9 us
  Pallas kernels  24.2 us (93%)
  local copies, waits for them, and re-layouts  1.67 us (6%)
    pallas_call x1, Pallas kernels, body(): pl.pallas_call(kernel, out_shape=jax.ShapeDtypeStruct(shape, f32), in_spe...  24.2 us
    unnamed x1, local copies, waits for them, and re-layouts  1.67 us

commit v1 on v0

--- a/solution.py
+++ b/solution.py
@@ -204,11 +204,11 @@
     odd_y = (y_at & 1) == 1
     odd_z = (z_at & 1) == 1
 
-    def loop(lo, hi, step, unroll=4):
+    def loop(lo, hi, step):
         def run(i, carry):
             step(i)
             return carry
-        lax.fori_loop(lo, hi, run, 0, unroll=unroll)
+        lax.fori_loop(lo, hi, run, 0, unroll=True)
 
     def set_rim(body, halo):
         for at, a, b, count in ((1, 3, 11, 8), (0, 1, 2, 1), (9, 19, 20, 1)):

time: 26.1 us -> 23.6 us (0.904)
  Pallas kernels: 24.2 us -> 21.7 us
    pallas_call x1, Pallas kernels: 24.2 us -> 21.7 us  [body(): pl.pallas_call(kernel, out_shape=jax.ShapeDtypeStruct(shape, f32), in_spe...]
where the time goes in v1:
time: 23.6 us; the launch traced here: 23.4 us
  Pallas kernels  21.7 us (92%)
  local copies, waits for them, and re-layouts  1.67 us (7%)
    pallas_call x1, Pallas kernels, body(): pl.pallas_call(kernel, out_shape=jax.ShapeDtypeStruct(shape, f32), in_spe...  21.7 us
    unnamed x1, local copies, waits for them, and re-layouts  1.67 us

profile of v1, /device:TPU:0, one launch (start us, length us, event | category | flops | bytes accessed | tf_op | source)
XLA Modules:
  0.0 23.4 jit_solution(8887840849309471634)
XLA Ops:
  0.0 21.7 %shard_map.46 = f32[16,16,256]{2,1,0:T(8,128)} custom-call(s32[64]{0:T(128)} %agg.1, f32[16,16,256]{2,1,0:T(8,128)} %k_in.1, f32[16,16,256]{2,1,0:T(8,128)} %s_in.1, f32[16,16,256]{2,1,0:T(8,128)} %p_in.1), custom_call_target="tpu_custom_call" | custom-call | tf_op jit(solution)/shard_map/pallas_call | solution.py:439
  21.7 1.7 %copy.6 = f32[16,16,256]{2,1,0:T(8,128)} copy(f32[16,16,256]{2,1,0:T(8,128)} %shard_map.46) | data formatting | bytes 524288

commit v2 on v1

--- a/solution.py
+++ b/solution.py
@@ -266,23 +266,39 @@
         for way in range(2):
             packed[way, pair, 0:a.shape[0]] = tiles[way].reshape(a.shape)
 
+    own, rim, every = slice(0, 16), slice(16, 24), slice(0, 24)
+
+    def x_faces(part):
+        def step(i):
+            fx[i, part] = face(ke[i, part], ke[i + 1, part])
+        return step
+
+    def z_faces(part):
+        def step(i):
+            k = ke[i, part]
+            fz[i, part] = jnp.where(z_at[part] == 255, 0.0, face(k, next_z(k)))
+        return step
+
+    loop(3, 18, x_faces(own))
+    loop(3, 19, z_faces(own))
     receive("k")
     set_rim(ke, khalo)
-
-    def x_faces(i):
-        fx[i] = face(ke[i], ke[i + 1])
-    loop(0, 21, x_faces)
+    loop(3, 18, x_faces(rim))
+    loop(3, 19, z_faces(rim))
+    for lo, hi in ((0, 3), (18, 21)):
+        loop(lo, hi, x_faces(every))
+    for lo, hi in ((1, 3), (19, 21)):
+        loop(lo, hi, z_faces(every))
 
     def other_faces(i):
         k = ke[i]
         north = face(k, next_y(k))
-        above = jnp.where(z_at == 255, 0.0, face(k, next_z(k)))
+        above = fz[i]
         south, below = prev_y(north), prev_z(above)
         x_glob = slab * width + i - 3
         ends_x = (x_glob == 0).astype(f32) + (x_glob == slabs * width - 1).astype(f32)
         bound = 2.0 * k * (ends_yz + ends_x)
         fy[i] = north
-        fz[i] = above
         diag = fx[i - 1] + fx[i] + north + south + above + below + bound
         dg[i] = diag
         wt[i] = OMEGA / jnp.where(diag > 0, diag, 1.0)

time: 23.6 us -> 23.4 us (level)
  no operation moved by 1% of the time
where the time goes in v2:
time: 23.4 us; the launch traced here: 23.3 us
  Pallas kernels  21.6 us (92%)
  local copies, waits for them, and re-layouts  1.67 us (7%)
    pallas_call x1, Pallas kernels, body(): pl.pallas_call(kernel, out_shape=jax.ShapeDtypeStruct(shape, f32), in_spe...  21.6 us
    unnamed x1, local copies, waits for them, and re-layouts  1.67 us

profile of v2, /device:TPU:0, one launch (start us, length us, event | category | flops | bytes accessed | tf_op | source)
XLA Modules:
  0.0 23.3 jit_solution(2335471551534126601)
XLA Ops:
  0.0 21.6 %shard_map.46 = f32[16,16,256]{2,1,0:T(8,128)} custom-call(s32[64]{0:T(128)} %agg.1, f32[16,16,256]{2,1,0:T(8,128)} %k_in.1, f32[16,16,256]{2,1,0:T(8,128)} %s_in.1, f32[16,16,256]{2,1,0:T(8,128)} %p_in.1), custom_call_target="tpu_custom_call" | custom-call | tf_op jit(solution)/shard_map/pallas_call | solution.py:455
  21.6 1.7 %copy.6 = f32[16,16,256]{2,1,0:T(8,128)} copy(f32[16,16,256]{2,1,0:T(8,128)} %shard_map.46) | data formatting | bytes 524288
